TPU v7x, 32 devices: a whole 2x2x4 slice. The times are simulated.
32 devices in a mesh: layer: 8 (over z, x), shot: 4 (over y, core).
Axes of the slice: x: 2, y: 2, z: 4, core: 2. Of those that a mesh axis runs over, the one named last changes fastest.
Arguments:
- down_state: bfloat16 [8, 1024, 2048], P('layer', None, 'shot'), may hold values from -6 to 6
- up_state: bfloat16 [8, 1024, 2048], P('layer', None, 'shot'), may hold values from -6 to 6
- down_op: bfloat16 [8, 1024, 1024], P('layer', 'shot'), may hold values from -0.1875 to 0.1875
- up_op: bfloat16 [8, 1024, 1024], P('layer', 'shot'), may hold values from -0.1875 to 0.1875
- reflect_op: bfloat16 [8, 1024, 1024], P('layer', 'shot'), may hold values from -0.125 to 0.125
- source_bank: bfloat16 [8, 2, 1024, 2048], P('layer', None, None, 'shot'), may hold values from -4 to 4
- plan: int32 [4, 8], P(None, 'layer'), may hold values from 0 to 1
- layer_source: int32 [8], P('layer'), may hold values from 0 to 1
Outputs:
- down_out: bfloat16 [8, 1024, 2048], P('layer', None, 'shot')
- up_out: bfloat16 [8, 1024, 2048], P('layer', None, 'shot')
All inputs are finite; a program needn't handle non-finite values.
Results may differ from a plain program's by a relative error of at most 0.008.
Values may be sent and summed in bfloat16 or wider, within the bound.
A program may use at most 64 MiB of HBM per device.

v0:
```python
import jax
import jax.numpy as jnp
from jax import lax
from jax.sharding import PartitionSpec as P

TICKS = 4


def passed_along(value, axis, steps):
    count = lax.axis_size(axis)
    leading, last = (max(0, -steps), min(count, count - steps))
    return lax.ppermute(value, axis, [(source, source + steps) for source in range(leading, last)])


def body(down_state, up_state, down_op, up_op, reflect_op, source_bank, plan, layer_source):
    sources = source_bank[0]
    upward_source = lax.dynamic_index_in_dim(sources, layer_source[0], 0, keepdims=False)
    downgoing = down_state[0]
    upgoing = up_state[0]
    full_down, full_up, full_reflect = (
        lax.all_gather(down_op[0], "shot", axis=0, tiled=True),
        lax.all_gather(up_op[0], "shot", axis=0, tiled=True),
        lax.all_gather(reflect_op[0], "shot", axis=0, tiled=True),
    )
    for moment in range(TICKS):
        injected = lax.dynamic_index_in_dim(sources, plan[moment, 0], 0, keepdims=False)
        received_down = passed_along(downgoing, "layer", 1)
        received_up = passed_along(upgoing, "layer", -1)
        down_in = (received_down.astype(jnp.float32) + injected.astype(jnp.float32)).astype(
            jnp.bfloat16
        )
        new_down = jnp.dot(full_down, down_in, preferred_element_type=jnp.float32).astype(
            jnp.bfloat16
        )
        total = jnp.dot(full_up, received_up, preferred_element_type=jnp.float32)
        total = total + jnp.dot(full_reflect, down_in, preferred_element_type=jnp.float32)
        total = total + upward_source.astype(jnp.float32)
        downgoing = new_down
        upgoing = total.astype(jnp.bfloat16)
    return (downgoing[None], upgoing[None])


def solution(mesh):
    placed = (
        P("layer", None, "shot"),
        P("layer", None, "shot"),
        P("layer", "shot", None),
        P("layer", "shot", None),
        P("layer", "shot", None),
        P("layer", None, None, "shot"),
        P(None, "layer"),
        P("layer"),
    )
    return jax.shard_map(
        body,
        mesh=mesh,
        in_specs=placed,
        out_specs=(P("layer", None, "shot"), P("layer", None, "shot")),
        check_vma=False,
    )
```

profile of v0, /device:TPU:10, one launch (start us, length us, event | category | flops | bytes accessed | tf_op | source)
XLA Modules:
  0.0 229.1 jit_solution(4420387766130614906)
XLA Ops:
  7.9 0.7 all-gather.11.cloned.1.call-update
  9.4 3.5 %collective-permute-start = (bf16[1024,512]{1,0:T(8,128)(2,1)}, bf16[1024,512]{1,0:T(8,128)(2,1)}, u32[]{:S(2)}, u32[]{:S(2)}) collective-permute-start(bf16[1024,512]{1,0:T(8,128)(2,1)} %bitcast.117), channel_id=1, source_target_pairs={{0,4},{4,8},{8,12},{12,16},{16,20},{20,24},{24,28},{1,5},{5,9},{9,... | collective-permute-start | bytes 3145736 | tf_op jit(solution)/shard_map/ppermute | solution.py:12
  12.8 2.4 %collective-permute-start.4 = (bf16[1024,512]{1,0:T(8,128)(2,1)}, bf16[1024,512]{1,0:T(8,128)(2,1)}, u32[]{:S(2)}, u32[]{:S(2)}) collective-permute-start(bf16[1024,512]{1,0:T(8,128)(2,1)} %bitcast.118), channel_id=1, source_target_pairs={{4,0},{8,4},{12,8},{16,12},{20,16},{24,20},{28,24},{5,1},{9,5},{13... | collective-permute-start | bytes 3145736 | tf_op jit(solution)/shard_map/ppermute | solution.py:12
  15.2 1.4 fusion.77
  24.0 4.0 %constant_dynamic-slice_fusion = (bf16[1,1,1024,512]{3,2,1,0:T(8,128)(2,1)}, bf16[1,1,1024,512]{3,2,1,0:T(8,128)(2,1)S(1)}, bf16[1,1,1024,512]{3,2,1,0:T(8,128)(2,1)}, bf16[1,1,1024,512]{3,2,1,0:T(8,128)(2,1)}) fusion(bf16[1,2,1024,512]{3,2,1,0:T(8,128)(2,1)} %param.13, s32[]{:T(128)S(6)} %select_n.20, s32[]{:T(128)S(6)} %select_n.19, s32[]{:T(128)S(6)} %select_n.18, ...), kind=kLoop, calls=%fused_computation.51 | loop fusion | bytes 8388624 | tf_op jit(solution)/shard_map/jit(dynamic_index_in_dim)/dynamic_slice | solution.py:17
  28.1 2.5 %copy.19 = bf16[1,1,1024,512]{2,3,1,0:T(8,128)(2,1)} copy(bf16[1,1,1024,512]{3,2,1,0:T(8,128)(2,1)} %get-tuple-element.4) | data formatting | bytes 2097152
  31.1 27.8 %collective-permute-done = bf16[1024,512]{1,0:T(8,128)(2,1)} collective-permute-done((bf16[1024,512]{1,0:T(8,128)(2,1)}, bf16[1024,512]{1,0:T(8,128)(2,1)}, u32[]{:S(2)}, u32[]{:S(2)}) %collective-permute-start) | collective-permute-done | bytes 1048608 | tf_op jit(solution)/shard_map/ppermute | solution.py:12
  59.0 4.2 %fusion.59 = bf16[1024,512]{0,1:T(8,128)(2,1)} fusion(bf16[1,1024,1024]{2,1,0:T(8,128)(2,1)} %all-gather.7.cloned.1.call-done, bf16[1024,512]{1,0:T(8,128)(2,1)} %collective-permute-done, bf16[1,2,1024,512]{3,2,1,0:T(8,128)(2,1)S(1)} %copy-done, s32[]{:T(128)S(6)} %select_n.16), kind=kOutput, calls=%fused_computation.48 | convolution fusion | flops 1076363264 | bytes 5242884 | tf_op jit(solution)/shard_map/dot_general | solution.py:32
  63.2 2.5 %collective-permute-start.1 = (bf16[1024,512]{0,1:T(8,128)(2,1)}, bf16[1024,512]{0,1:T(8,128)(2,1)}, u32[]{:S(2)}, u32[]{:S(2)}) collective-permute-start(bf16[1024,512]{0,1:T(8,128)(2,1)} %fusion.59), channel_id=1, source_target_pairs={{0,4},{4,8},{8,12},{12,16},{16,20},{20,24},{24,28},{1,5},{5,9},{9,... | collective-permute-start | bytes 3145736 | tf_op jit(solution)/shard_map/ppermute | solution.py:12
  65.7 4.8 %fusion.14 = f32[512,1024]{1,0:T(8,128)} fusion(bf16[1,1024,1024]{2,1,0:T(8,128)(2,1)} %all-gather.11.cloned.1.call-done, bf16[1024,512]{1,0:T(8,128)(2,1)} %collective-permute-done, bf16[1,2,1024,512]{3,2,1,0:T(8,128)(2,1)S(1)} %copy-done, s32[]{:T(128)S(6)} %select_n.16), kind=kOutput, calls=%fused_computation.23 | convolution fusion | flops 1075838976 | bytes 6291460 | tf_op jit(solution)/shard_map/dot_general | solution.py:36
  70.5 11.2 %all-gather.9.cloned.1.call-done = bf16[1,1024,1024]{2,1,0:T(8,128)(2,1)} async-done(((bf16[1,256,1024]{2,1,0:T(8,128)(2,1)}), bf16[1,1024,1024]{2,1,0:T(8,128)(2,1)}) %all-gather.9.cloned.1.call-update) | async-done | bytes 2097168 | tf_op jit(solution)/shard_map/all_gather | solution.py:22
  81.7 5.2 %fusion = bf16[1024,512]{0,1:T(8,128)(2,1)} fusion(f32[512,1024]{1,0:T(8,128)} %fusion.14, bf16[1024,512]{1,0:T(8,128)(2,1)} %collective-permute-done.4, bf16[1,1024,1024]{2,1,0:T(8,128)(2,1)} %all-gather.9.cloned.1.call-done, bf16[1,1,1024,512]{2,3,1,0:T(8,128)(2,1)} %copy.19), kind=kOutput, calls=%fused_computation.4 | convolution fusion | flops 1075838976 | bytes 7340032 | tf_op jit(solution)/shard_map/dot_general | solution.py:35
  86.9 2.5 %collective-permute-start.5 = (bf16[1024,512]{0,1:T(8,128)(2,1)}, bf16[1024,512]{0,1:T(8,128)(2,1)}, u32[]{:S(2)}, u32[]{:S(2)}) collective-permute-start(bf16[1024,512]{0,1:T(8,128)(2,1)} %fusion), channel_id=1, source_target_pairs={{4,0},{8,4},{12,8},{16,12},{20,16},{24,20},{28,24},{5,1},{9,5},{13... | collective-permute-start | bytes 3145736 | tf_op jit(solution)/shard_map/ppermute | solution.py:12
  89.9 4.3 %fusion.56 = bf16[1024,512]{0,1:T(8,128)(2,1)} fusion(bf16[1,1024,1024]{2,1,0:T(8,128)(2,1)} %all-gather.7.cloned.1.call-done, bf16[1024,512]{0,1:T(8,128)(2,1)} %collective-permute-done.1, bf16[1,1,1024,512]{2,3,1,0:T(8,128)(2,1)S(1)} %copy.16), kind=kOutput, calls=%fused_computation.47 | convolution fusion | flops 1076363264 | bytes 5242880 | tf_op jit(solution)/shard_map/dot_general | solution.py:32
  94.2 4.5 %collective-permute-start.2 = (bf16[1024,512]{0,1:T(8,128)(2,1)}, bf16[1024,512]{0,1:T(8,128)(2,1)}, u32[]{:S(2)}, u32[]{:S(2)}) collective-permute-start(bf16[1024,512]{0,1:T(8,128)(2,1)} %fusion.56), channel_id=1, source_target_pairs={{0,4},{4,8},{8,12},{12,16},{16,20},{20,24},{24,28},{1,5},{5,9},{9,... | collective-permute-start | bytes 3145736 | tf_op jit(solution)/shard_map/ppermute | solution.py:12
  98.8 2.5 %fusion.12 = f32[512,1024]{1,0:T(8,128)S(1)} fusion(bf16[1,1024,1024]{2,1,0:T(8,128)(2,1)S(1)} %copy-done.5, bf16[1024,512]{0,1:T(8,128)(2,1)} %collective-permute-done.1, bf16[1,1,1024,512]{2,3,1,0:T(8,128)(2,1)S(1)} %copy.16), kind=kOutput, calls=%fused_computation.21 | convolution fusion | flops 1075838976 | bytes 6291456 | tf_op jit(solution)/shard_map/dot_general | solution.py:36
  101.3 33.6 %collective-permute-done.5 = bf16[1024,512]{0,1:T(8,128)(2,1)} collective-permute-done((bf16[1024,512]{0,1:T(8,128)(2,1)}, bf16[1024,512]{0,1:T(8,128)(2,1)}, u32[]{:S(2)}, u32[]{:S(2)}) %collective-permute-start.5) | collective-permute-done | bytes 1048608 | tf_op jit(solution)/shard_map/ppermute | solution.py:12
  134.9 3.6 %fusion.1 = bf16[1024,512]{0,1:T(8,128)(2,1)} fusion(f32[512,1024]{1,0:T(8,128)S(1)} %fusion.12, bf16[1024,512]{0,1:T(8,128)(2,1)} %collective-permute-done.5, bf16[1,1024,1024]{2,1,0:T(8,128)(2,1)S(1)} %copy-done.7, bf16[1,1,1024,512]{2,3,1,0:T(8,128)(2,1)S(1)} %copy-done.3), kind=kOutput, calls=%fused_computation.5 | convolution fusion | flops 1075838976 | bytes 7340032 | tf_op jit(solution)/shard_map/dot_general | solution.py:35
  138.5 4.4 %collective-permute-start.6 = (bf16[1024,512]{0,1:T(8,128)(2,1)}, bf16[1024,512]{0,1:T(8,128)(2,1)}, u32[]{:S(2)}, u32[]{:S(2)}) collective-permute-start(bf16[1024,512]{0,1:T(8,128)(2,1)} %fusion.1), channel_id=1, source_target_pairs={{4,0},{8,4},{12,8},{16,12},{20,16},{24,20},{28,24},{5,1},{9,5},{13... | collective-permute-start | bytes 3145736 | tf_op jit(solution)/shard_map/ppermute | solution.py:12
  142.9 1.3 copy.17
  144.3 4.6 %fusion.53 = bf16[1024,512]{0,1:T(8,128)(2,1)} fusion(bf16[1,1024,1024]{2,1,0:T(8,128)(2,1)} %all-gather.7.cloned.1.call-done, bf16[1024,512]{0,1:T(8,128)(2,1)} %collective-permute-done.2, bf16[1,1,1024,512]{2,3,1,0:T(8,128)(2,1)} %copy.17), kind=kOutput, calls=%fused_computation.46 | convolution fusion | flops 1076363264 | bytes 5242880 | tf_op jit(solution)/shard_map/dot_general | solution.py:32
  148.9 3.1 %collective-permute-start.3 = (bf16[1024,512]{0,1:T(8,128)(2,1)}, bf16[1024,512]{0,1:T(8,128)(2,1)}, u32[]{:S(2)}, u32[]{:S(2)}) collective-permute-start(bf16[1024,512]{0,1:T(8,128)(2,1)} %fusion.53), channel_id=1, source_target_pairs={{0,4},{4,8},{8,12},{12,16},{16,20},{20,24},{24,28},{1,5},{5,9},{9,... | collective-permute-start | bytes 3145736 | tf_op jit(solution)/shard_map/ppermute | solution.py:12
  152.1 2.5 %fusion.10 = f32[512,1024]{1,0:T(8,128)S(1)} fusion(bf16[1,1024,1024]{2,1,0:T(8,128)(2,1)S(1)} %copy-done.6, bf16[1024,512]{0,1:T(8,128)(2,1)} %collective-permute-done.2, bf16[1,1,1024,512]{2,3,1,0:T(8,128)(2,1)S(1)} %copy-done.4), kind=kOutput, calls=%fused_computation.19 | convolution fusion | flops 1075838976 | bytes 6291456 | tf_op jit(solution)/shard_map/dot_general | solution.py:36
  154.6 33.1 %collective-permute-done.6 = bf16[1024,512]{0,1:T(8,128)(2,1)} collective-permute-done((bf16[1024,512]{0,1:T(8,128)(2,1)}, bf16[1024,512]{0,1:T(8,128)(2,1)}, u32[]{:S(2)}, u32[]{:S(2)}) %collective-permute-start.6) | collective-permute-done | bytes 1048608 | tf_op jit(solution)/shard_map/ppermute | solution.py:12
  187.7 3.5 %fusion.2 = bf16[1024,512]{0,1:T(8,128)(2,1)} fusion(f32[512,1024]{1,0:T(8,128)S(1)} %fusion.10, bf16[1024,512]{0,1:T(8,128)(2,1)} %collective-permute-done.6, bf16[1,1024,1024]{2,1,0:T(8,128)(2,1)S(1)} %copy-done.8, bf16[1,1,1024,512]{2,3,1,0:T(8,128)(2,1)S(1)} %copy-done.3), kind=kOutput, calls=%fused_computation.6 | convolution fusion | flops 1075838976 | bytes 7340032 | tf_op jit(solution)/shard_map/dot_general | solution.py:35
  191.2 4.4 %collective-permute-start.7 = (bf16[1024,512]{0,1:T(8,128)(2,1)}, bf16[1024,512]{0,1:T(8,128)(2,1)}, u32[]{:S(2)}, u32[]{:S(2)}) collective-permute-start(bf16[1024,512]{0,1:T(8,128)(2,1)} %fusion.2), channel_id=1, source_target_pairs={{4,0},{8,4},{12,8},{16,12},{20,16},{24,20},{28,24},{5,1},{9,5},{13... | collective-permute-start | bytes 3145736 | tf_op jit(solution)/shard_map/ppermute | solution.py:12
  196.2 3.2 %fusion.50 = bf16[1,1024,512]{1,2,0:T(8,128)(2,1)S(1)} fusion(bf16[1,1024,1024]{2,1,0:T(8,128)(2,1)} %all-gather.7.cloned.1.call-done, bf16[1024,512]{0,1:T(8,128)(2,1)} %collective-permute-done.3, bf16[1,1,1024,512]{2,3,1,0:T(8,128)(2,1)S(1)} %copy.18), kind=kOutput, calls=%fused_computation.45 | convolution fusion | flops 1076363264 | bytes 5242880 | tf_op jit(solution)/shard_map/dot_general | solution.py:32
  199.4 1.3 copy.14
  200.7 3.3 %fusion.8 = f32[512,1024]{1,0:T(8,128)S(1)} fusion(bf16[1,1024,1024]{2,1,0:T(8,128)(2,1)} %all-gather.11.cloned.1.call-done, bf16[1024,512]{0,1:T(8,128)(2,1)} %collective-permute-done.3, bf16[1,1,1024,512]{2,3,1,0:T(8,128)(2,1)S(1)} %copy.18), kind=kOutput, calls=%fused_computation.17 | convolution fusion | flops 1075838976 | bytes 6291456 | tf_op jit(solution)/shard_map/dot_general | solution.py:36
  204.0 14.6 %collective-permute-done.7 = bf16[1024,512]{0,1:T(8,128)(2,1)} collective-permute-done((bf16[1024,512]{0,1:T(8,128)(2,1)}, bf16[1024,512]{0,1:T(8,128)(2,1)}, u32[]{:S(2)}, u32[]{:S(2)}) %collective-permute-start.7) | collective-permute-done | bytes 1048608 | tf_op jit(solution)/shard_map/ppermute | solution.py:12
  218.6 2.6 %fusion.62 = bf16[1,1024,512]{1,2,0:T(8,128)(2,1)S(1)} fusion(f32[512,1024]{1,0:T(8,128)S(1)} %fusion.8, bf16[1024,512]{0,1:T(8,128)(2,1)} %collective-permute-done.7, bf16[1,1024,1024]{2,1,0:T(8,128)(2,1)S(1)} %copy-done.9, bf16[1,1,1024,512]{2,3,1,0:T(8,128)(2,1)S(1)} %copy-done.3), kind=kOutput, calls=%fused_computation.49 | convolution fusion | flops 1075838976 | bytes 7340032 | tf_op jit(solution)/shard_map/dot_general | solution.py:35
  221.2 1.3 copy.15
  (33 shorter events, 2.6 us)
Async XLA Ops:
  7.2 51.8 %all-gather.7.cloned.1.call-start = ((), (), s32[]{:S(2)}) async-start(), calls=%async_computation | async-start | bytes 2621440 | tf_op jit(solution)/shard_map/all_gather | solution.py:21
  7.9 57.8 %all-gather.11.cloned.1.call-start = ((), (), s32[]{:S(2)}) async-start(), calls=%async_computation.2 | async-start | bytes 2621440 | tf_op jit(solution)/shard_map/all_gather | solution.py:23
  8.6 73.0 %all-gather.9.cloned.1.call-start = ((), (), s32[]{:S(2)}) async-start(), calls=%async_computation.1 | async-start | bytes 2621440 | tf_op jit(solution)/shard_map/all_gather | solution.py:22
  9.4 49.6 %collective-permute-start = (bf16[1024,512]{1,0:T(8,128)(2,1)}, bf16[1024,512]{1,0:T(8,128)(2,1)}, u32[]{:S(2)}, u32[]{:S(2)}) collective-permute-start(bf16[1024,512]{1,0:T(8,128)(2,1)} %bitcast.117), channel_id=1, source_target_pairs={{0,4},{4,8},{8,12},{12,16},{16,20},{20,24},{24,28},{1,5},{5,9},{9,... | collective-permute-start | bytes 3145736 | tf_op jit(solution)/shard_map/ppermute | solution.py:12
  12.8 57.7 %collective-permute-start.4 = (bf16[1024,512]{1,0:T(8,128)(2,1)}, bf16[1024,512]{1,0:T(8,128)(2,1)}, u32[]{:S(2)}, u32[]{:S(2)}) collective-permute-start(bf16[1024,512]{1,0:T(8,128)(2,1)} %bitcast.118), channel_id=1, source_target_pairs={{4,0},{8,4},{12,8},{16,12},{20,16},{24,20},{28,24},{5,1},{9,5},{13... | collective-permute-start | bytes 3145736 | tf_op jit(solution)/shard_map/ppermute | solution.py:12
  28.1 30.9 %copy-start = (bf16[1,2,1024,512]{3,2,1,0:T(8,128)(2,1)S(1)}, bf16[1,2,1024,512]{3,2,1,0:T(8,128)(2,1)}, u32[]{:S(2)}) copy-start(bf16[1,2,1024,512]{3,2,1,0:T(8,128)(2,1)} %param.13) | copy-start | bytes 6291460
  63.2 26.7 %collective-permute-start.1 = (bf16[1024,512]{0,1:T(8,128)(2,1)}, bf16[1024,512]{0,1:T(8,128)(2,1)}, u32[]{:S(2)}, u32[]{:S(2)}) collective-permute-start(bf16[1024,512]{0,1:T(8,128)(2,1)} %fusion.59), channel_id=1, source_target_pairs={{0,4},{4,8},{8,12},{12,16},{16,20},{20,24},{24,28},{1,5},{5,9},{9,... | collective-permute-start | bytes 3145736 | tf_op jit(solution)/shard_map/ppermute | solution.py:12
  70.5 18.8 %copy-start.2 = (bf16[1,1,1024,512]{3,2,1,0:T(8,128)(2,1)S(1)}, bf16[1,1,1024,512]{3,2,1,0:T(8,128)(2,1)}, u32[]{:S(2)}) copy-start(bf16[1,1,1024,512]{3,2,1,0:T(8,128)(2,1)} %get-tuple-element.7) | copy-start | bytes 3145732
  86.9 48.0 %collective-permute-start.5 = (bf16[1024,512]{0,1:T(8,128)(2,1)}, bf16[1024,512]{0,1:T(8,128)(2,1)}, u32[]{:S(2)}, u32[]{:S(2)}) collective-permute-start(bf16[1024,512]{0,1:T(8,128)(2,1)} %fusion), channel_id=1, source_target_pairs={{4,0},{8,4},{12,8},{16,12},{20,16},{24,20},{28,24},{5,1},{9,5},{13... | collective-permute-start | bytes 3145736 | tf_op jit(solution)/shard_map/ppermute | solution.py:12
  89.9 8.9 %copy-start.5 = (bf16[1,1024,1024]{2,1,0:T(8,128)(2,1)S(1)}, bf16[1,1024,1024]{2,1,0:T(8,128)(2,1)}, u32[]{:S(2)}) copy-start(bf16[1,1024,1024]{2,1,0:T(8,128)(2,1)} %all-gather.11.cloned.1.call-done) | copy-start | bytes 6291460
  94.2 40.7 %copy-start.3 = (bf16[1,1,1024,512]{2,3,1,0:T(8,128)(2,1)S(1)}, bf16[1,1,1024,512]{2,3,1,0:T(8,128)(2,1)}, u32[]{:S(2)}) copy-start(bf16[1,1,1024,512]{2,3,1,0:T(8,128)(2,1)} %copy.19) | copy-start | bytes 3145732
  94.2 40.7 %copy-start.7 = (bf16[1,1024,1024]{2,1,0:T(8,128)(2,1)S(1)}, bf16[1,1024,1024]{2,1,0:T(8,128)(2,1)}, u32[]{:S(2)}) copy-start(bf16[1,1024,1024]{2,1,0:T(8,128)(2,1)} %all-gather.9.cloned.1.call-done) | copy-start | bytes 6291460
  94.2 50.0 %collective-permute-start.2 = (bf16[1024,512]{0,1:T(8,128)(2,1)}, bf16[1024,512]{0,1:T(8,128)(2,1)}, u32[]{:S(2)}, u32[]{:S(2)}) collective-permute-start(bf16[1024,512]{0,1:T(8,128)(2,1)} %fusion.56), channel_id=1, source_target_pairs={{0,4},{4,8},{8,12},{12,16},{16,20},{20,24},{24,28},{1,5},{5,9},{9,... | collective-permute-start | bytes 3145736 | tf_op jit(solution)/shard_map/ppermute | solution.py:12
  101.3 41.6 %copy-start.1 = (bf16[1,1,1024,512]{3,2,1,0:T(8,128)(2,1)S(1)}, bf16[1,1,1024,512]{3,2,1,0:T(8,128)(2,1)}, u32[]{:S(2)}) copy-start(bf16[1,1,1024,512]{3,2,1,0:T(8,128)(2,1)} %get-tuple-element.6) | copy-start | bytes 3145732
  138.5 49.2 %collective-permute-start.6 = (bf16[1024,512]{0,1:T(8,128)(2,1)}, bf16[1024,512]{0,1:T(8,128)(2,1)}, u32[]{:S(2)}, u32[]{:S(2)}) collective-permute-start(bf16[1024,512]{0,1:T(8,128)(2,1)} %fusion.1), channel_id=1, source_target_pairs={{4,0},{8,4},{12,8},{16,12},{20,16},{24,20},{28,24},{5,1},{9,5},{13... | collective-permute-start | bytes 3145736 | tf_op jit(solution)/shard_map/ppermute | solution.py:12
  144.2 7.8 %copy-start.4 = (bf16[1,1,1024,512]{2,3,1,0:T(8,128)(2,1)S(1)}, bf16[1,1,1024,512]{2,3,1,0:T(8,128)(2,1)}, u32[]{:S(2)}) copy-start(bf16[1,1,1024,512]{2,3,1,0:T(8,128)(2,1)} %copy.17) | copy-start | bytes 3145732
  144.2 7.8 %copy-start.6 = (bf16[1,1024,1024]{2,1,0:T(8,128)(2,1)S(1)}, bf16[1,1024,1024]{2,1,0:T(8,128)(2,1)}, u32[]{:S(2)}) copy-start(bf16[1,1024,1024]{2,1,0:T(8,128)(2,1)} %all-gather.11.cloned.1.call-done) | copy-start | bytes 6291460
  148.9 38.8 %copy-start.8 = (bf16[1,1024,1024]{2,1,0:T(8,128)(2,1)S(1)}, bf16[1,1024,1024]{2,1,0:T(8,128)(2,1)}, u32[]{:S(2)}) copy-start(bf16[1,1024,1024]{2,1,0:T(8,128)(2,1)} %all-gather.9.cloned.1.call-done) | copy-start | bytes 6291460
  148.9 47.2 %collective-permute-start.3 = (bf16[1024,512]{0,1:T(8,128)(2,1)}, bf16[1024,512]{0,1:T(8,128)(2,1)}, u32[]{:S(2)}, u32[]{:S(2)}) collective-permute-start(bf16[1024,512]{0,1:T(8,128)(2,1)} %fusion.53), channel_id=1, source_target_pairs={{0,4},{4,8},{8,12},{12,16},{16,20},{20,24},{24,28},{1,5},{5,9},{9,... | collective-permute-start | bytes 3145736 | tf_op jit(solution)/shard_map/ppermute | solution.py:12
  191.2 27.4 %collective-permute-start.7 = (bf16[1024,512]{0,1:T(8,128)(2,1)}, bf16[1024,512]{0,1:T(8,128)(2,1)}, u32[]{:S(2)}, u32[]{:S(2)}) collective-permute-start(bf16[1024,512]{0,1:T(8,128)(2,1)} %fusion.2), channel_id=1, source_target_pairs={{4,0},{8,4},{12,8},{16,12},{20,16},{24,20},{28,24},{5,1},{9,5},{13... | collective-permute-start | bytes 3145736 | tf_op jit(solution)/shard_map/ppermute | solution.py:12
  200.7 18.0 %copy-start.9 = (bf16[1,1024,1024]{2,1,0:T(8,128)(2,1)S(1)}, bf16[1,1024,1024]{2,1,0:T(8,128)(2,1)}, u32[]{:S(2)}) copy-start(bf16[1,1024,1024]{2,1,0:T(8,128)(2,1)} %all-gather.9.cloned.1.call-done) | copy-start | bytes 6291460
Sparse Core Ops, SparseCore 0:
  9.6 23.7 all-gather.6
  34.9 22.5 all-gather.10
  59.1 22.5 all-gather.8
where the time goes:
time: 230 us; the launch traced here: 229 us
  waiting for transfers between devices  122 us (53%)
  matrix products  44.5 us (19%)
  starting transfers between devices  27.3 us (12%)
  between operations  21.9 us (10%)
  local copies, waits for them, and re-layouts  13 us (6%)
    ppermute x8, waiting for transfers between devices, passed_along(): lax.ppermute(value, axis, [(source, source + steps) for source in range(l...  109 us
    ppermute x8, starting transfers between devices, passed_along(): lax.ppermute(value, axis, [(source, source + steps) for source in range(l...  27.2 us
    dot_general x4, matrix products, body(): jnp.dot(full_down, down_in, preferred_element_type=jnp.float32)  16.4 us
    dot_general x4, matrix products, body(): total = jnp.dot(full_up, received_up, preferred_element_type=jnp.float32)  14.9 us
    dot_general x4, matrix products, body(): jnp.dot(full_reflect, down_in, preferred_element_type=jnp.float32)  13.2 us
    all_gather x1, waiting for transfers between devices, body(): lax.all_gather(up_op[0], 'shot', axis=0, tiled=True)  11.2 us
    unnamed x26, local copies, waits for them, and re-layouts  7.58 us
  transfers between devices with their start and end apart: 11, of which 5 were waited for; matrix products, arithmetic and copies ran while one was open for 23% of the time, Pallas kernels for 0%

commit v1 on v0

v1 whole, which is shorter than its diff:
```python
import functools

import jax
import jax.numpy as jnp
from jax import lax
from jax.experimental import pallas as pl
from jax.experimental.pallas import tpu as pltpu
from jax.sharding import PartitionSpec as P

MESH = pl.DeviceIdType.MESH
LAG = 2


def low_bit(mask):
    return mask & -mask


def kernel(
    layers, shots, ticks, batches, chunks, width, tile,
    down_ref, up_ref, dop_ref, uop_ref, rop_ref, bank_ref, ctrl_ref,
    down_out, up_out,
    ops, inbuf, outbuf, bank, ctrl, mixed,
    xs, xr, cs, cr, ss, sr, gs, gr, zs, zr, lo, lt, lb, ls,
):
    me = lax.axis_index("layer")
    shot = lax.axis_index("shot")
    side = lax.rem(me, 2)
    mate = me + 1 - 2 * side
    order, block = ops.shape[2], dop_ref.shape[1]
    op_refs = (dop_ref, uop_ref, rop_ref)
    bits = [1 << i for i in reversed(range((shots - 1).bit_length()))]
    above, below = me + 2 < layers, me - 2 >= 0

    def rows(mask):
        return pl.ds(pl.multiple_of((shot ^ mask) * block, block), block)

    def cols(c):
        return pl.ds(pl.multiple_of(c * width, width), width)

    barrier = pltpu.get_barrier_semaphore()
    pl.semaphore_signal(barrier, inc=1, device_id=(mate, shot), device_id_type=MESH)
    for bit in bits:
        pl.semaphore_signal(barrier, inc=1, device_id=(me, shot ^ bit), device_id_type=MESH)

    @pl.when(above)
    def _():
        pl.semaphore_signal(barrier, inc=1, device_id=(me + 2, shot), device_id_type=MESH)

    @pl.when(below)
    def _():
        pl.semaphore_signal(barrier, inc=1, device_id=(me - 2, shot), device_id_type=MESH)

    local = []
    for k in range(3):
        local.append(pltpu.make_async_copy(op_refs[k].at[0], ops.at[0, k, rows(0)], lo.at[k]))
    for b in range(batches):
        for c in range(chunks):
            local.append(
                pltpu.make_async_copy(
                    bank_ref.at[0, b, :, pl.ds(c * width, width)], bank.at[0, b, c], lb.at[b, c]
                )
            )
    for copy in local:
        copy.start()

    def keep(c, which):
        source = up_ref if which else down_ref
        return pltpu.make_async_copy(source.at[0, :, cols(c)], inbuf.at[0, which, c], lt.at[c])

    for c in range(chunks):
        for which in (0, 1):
            pl.when(side == which)(keep(c, which).start)

    pl.semaphore_wait(barrier, 1 + len(bits) + above.astype(jnp.int32) + below.astype(jnp.int32))

    def cross(k):
        return pltpu.make_async_remote_copy(
            op_refs[k].at[0], ops.at[1, k, rows(0)], xs.at[k], xr.at[k],
            device_id=(mate, shot), device_id_type=MESH,
        )

    def spread(j, k, mask, bit):
        sem = (j, k, mask | bit)
        return pltpu.make_async_remote_copy(
            ops.at[j, k, rows(mask)], ops.at[j, k, rows(mask)], gs.at[sem], gr.at[sem],
            device_id=(me, shot ^ bit), device_id_type=MESH,
        )

    def arrived(j, k, mask):
        pltpu.make_async_copy(ops.at[j, k, rows(mask)], ops.at[j, k, rows(mask)], gr.at[j, k, mask]).wait()

    def onward(mask):
        return [bit for bit in bits if mask == 0 or bit < low_bit(mask)]

    relayed = [mask for mask in range(1, shots) if onward(mask)]
    relayed.sort(key=lambda mask: -low_bit(mask))
    settled = [mask for mask in range(1, shots) if not onward(mask)]

    def sources(b, c):
        return pltpu.make_async_remote_copy(
            bank_ref.at[0, b, :, cols(c)], bank.at[1, b, c], ss.at[b, c], sr.at[b, c],
            device_id=(mate, shot), device_id_type=MESH,
        )

    def first_to(which, c):
        source = up_ref if which else down_ref
        return pltpu.make_async_remote_copy(
            source.at[0, :, cols(c)], inbuf.at[0, which, c], zs.at[0, c], zr.at[0, c],
            device_id=(me + 2 - 4 * which, shot), device_id_type=MESH,
        )

    def pass_on(t, which, c):
        return pltpu.make_async_remote_copy(
            outbuf.at[t, c], inbuf.at[t + 1, which, c], zs.at[t + 1, c], zr.at[t + 1, c],
            device_id=(me + 2 - 4 * which, shot), device_id_type=MESH,
        )

    own_ctrl = pltpu.make_async_remote_copy(
        ctrl_ref, ctrl, cs, cr, device_id=(mate, shot), device_id_type=MESH
    )
    own_ctrl.start()
    for k in range(3):
        cross(k).start()
    for c in range(chunks):
        pl.when((side == 1) & above)(first_to(0, c).start)
        pl.when((side == 0) & below)(first_to(1, c).start)
    for k in range(3):
        local[k].wait()
        for bit in bits:
            if k == 0 or bit != bits[0]:
                spread(0, k, 0, bit).start()
    for k in range(3):
        cross(k).wait_recv()
        for bit in bits:
            spread(1, k, 0, bit).start()
    for b in range(batches):
        sources(b, 0).start()
    for mask in relayed:
        for k in range(3):
            arrived(1, k, mask)
            for bit in onward(mask):
                spread(1, k, mask, bit).start()
    for k in range(1, 3):
        spread(0, k, 0, bits[0]).start()
    for copy in local[3:]:
        copy.wait()
    for c in range(chunks):
        for which in (0, 1):
            pl.when(side == which)(keep(c, which).wait)
    own_ctrl.wait()
    for k in range(3):
        for mask in settled:
            arrived(1, k, mask)

    def picked(chosen, j, c, at):
        value = bank[j, 0, c, at, :].astype(jnp.float32)
        for b in range(1, batches):
            value = jnp.where(chosen == b, bank[j, b, c, at, :].astype(jnp.float32), value)
        return value

    def tick(t, c):
        even = lax.rem(t + side, 2) == 1
        j = 1 - lax.rem(t, 2)
        away = j == 1
        wanted = lambda row: jnp.where(away, ctrl[pl.ds(row, 1), :], ctrl_ref[pl.ds(row, 1), :])

        @pl.when(t == 0)
        def _():
            for b in range(batches):
                sources(b, c).wait_recv()

            @pl.when(c + 1 < chunks)
            def _():
                for b in range(batches):
                    sources(b, c + 1).start()

        @pl.when((t == 1) & (c == 0))
        def _():
            for mask in relayed:
                for k in range(3):
                    arrived(0, k, mask)
                    for bit in onward(mask):
                        spread(0, k, mask, bit).start()
            for k in range(3):
                for mask in settled:
                    arrived(0, k, mask)

        def mix():
            chosen = wanted(t)

            @pl.loop(0, order // tile)
            def _(r):
                at = pl.ds(pl.multiple_of(r * tile, tile), tile)
                value = inbuf[t, 0, c, at, :].astype(jnp.float32) + picked(chosen, j, c, at)
                mixed[at, :] = value.astype(mixed.dtype)

        def new_down(into):
            @pl.loop(0, order // tile)
            def _(r):
                at = pl.ds(pl.multiple_of(r * tile, tile), tile)
                total = jnp.dot(ops[j, 0, at, :], mixed[...], preferred_element_type=jnp.float32)
                into[at, :] = total.astype(into.dtype)

        def new_up(into):
            chosen = wanted(ticks)

            @pl.loop(0, order // tile)
            def _(r):
                at = pl.ds(pl.multiple_of(r * tile, tile), tile)
                total = jnp.dot(ops[j, 1, at, :], inbuf[t, 1, c], preferred_element_type=jnp.float32)
                total += jnp.dot(ops[j, 2, at, :], mixed[...], preferred_element_type=jnp.float32)
                total += picked(chosen, j, c, at)
                into[at, :] = total.astype(into.dtype)

        def received(which, there):
            @pl.when(there)
            def _():
                pltpu.make_async_copy(inbuf.at[t, which, c], inbuf.at[t, which, c], zr.at[t, c]).wait()

            @pl.when(jnp.logical_not(there))
            def _():
                inbuf[t, which, c] = jnp.zeros(inbuf.shape[3:], inbuf.dtype)

        more = t + 1 < ticks

        @pl.when(jnp.logical_not(even))
        def _():
            mix()
            new_down(outbuf.at[t, c])
            pl.when(more & above)(lambda: pass_on(t, 0, c).start())
            received(1, above)
            new_up(inbuf.at[t + 1, 1, c])

        @pl.when(even)
        def _():
            received(0, below)
            mix()
            new_up(outbuf.at[t, c])
            pl.when(more & below)(lambda: pass_on(t, 1, c).start())
            new_down(inbuf.at[t + 1, 0, c])

    @pl.loop(0, ticks + LAG * (chunks - 1))
    def _(i):
        @pl.loop(0, chunks)
        def _(c):
            t = i - LAG * c
            pl.when((t >= 0) & (t < ticks))(lambda: tick(t, c))

    last = ticks - 1
    ends_even = lax.rem(last + side, 2) == 1

    def results(kept_ref, sent_ref, which):
        made = []
        for c in range(chunks):
            at = pl.ds(c * width, width)
            made.append(pltpu.make_async_copy(inbuf.at[ticks, which, c], kept_ref.at[0, :, at], ls.at[0, c]))
            made.append(pltpu.make_async_copy(outbuf.at[last, c], sent_ref.at[0, :, at], ls.at[1, c]))
        for copy in made:
            copy.start()
        for copy in made:
            copy.wait()

    pl.when(ends_even)(lambda: results(down_out, up_out, 0))
    pl.when(jnp.logical_not(ends_even))(lambda: results(up_out, down_out, 1))

    for k in range(3):
        cross(k).wait_send()
    for j in range(2):
        for k in range(3):
            for mask in [0] + relayed:
                for bit in onward(mask):
                    spread(j, k, mask, bit).wait_send()
    for c in range(chunks):
        for b in range(batches):
            sources(b, c).wait_send()
        pl.when((side == 1) & above)(first_to(0, c).wait_send)
        pl.when((side == 0) & below)(first_to(1, c).wait_send)

    @pl.loop(0, ticks - 1)
    def _(t):
        even = lax.rem(t + side, 2) == 1
        for c in range(chunks):
            pl.when(even & below)(lambda: pass_on(t, 1, c).wait_send())
            pl.when(jnp.logical_not(even) & above)(lambda: pass_on(t, 0, c).wait_send())


def body(layers, shots, down_state, up_state, down_op, up_op, reflect_op, source_bank, plan, layer_source):
    order, columns = down_state.shape[1:]
    ticks, batches = plan.shape[0], source_bank.shape[1]
    width = 256 if columns % 256 == 0 else columns
    chunks = columns // width
    tile = 256 if order % 256 == 0 else order
    choices = jnp.concatenate([plan[:, 0], layer_source])
    depth = -(-choices.shape[0] // 8) * 8
    ctrl = jnp.broadcast_to(
        jnp.pad(choices, (0, depth - choices.shape[0]))[:, None], (depth, width)
    ).astype(jnp.int32)
    kind = down_state.dtype
    anywhere = pl.BlockSpec(memory_space=pl.ANY)
    dma = pltpu.SemaphoreType.DMA
    return pl.pallas_call(
        functools.partial(kernel, layers, shots, ticks, batches, chunks, width, tile),
        out_shape=(
            jax.ShapeDtypeStruct(down_state.shape, kind),
            jax.ShapeDtypeStruct(up_state.shape, kind),
        ),
        in_specs=[anywhere] * 6 + [pl.BlockSpec(memory_space=pltpu.VMEM)],
        out_specs=(anywhere, anywhere),
        scratch_shapes=[
            pltpu.VMEM((2, 3, order, order), kind),
            pltpu.VMEM((ticks + 1, 2, chunks, order, width), kind),
            pltpu.VMEM((ticks, chunks, order, width), kind),
            pltpu.VMEM((2, batches, chunks, order, width), kind),
            pltpu.VMEM((depth, width), jnp.int32),
            pltpu.VMEM((order, width), kind),
            dma((3,)), dma((3,)),
            dma, dma,
            dma((batches, chunks)), dma((batches, chunks)),
            dma((2, 3, shots)), dma((2, 3, shots)),
            dma((ticks, chunks)), dma((ticks, chunks)),
            dma((3,)), dma((chunks,)), dma((batches, chunks)), dma((2, chunks)),
        ],
        compiler_params=pltpu.CompilerParams(
            collective_id=0, has_side_effects=True, vmem_limit_bytes=56 * 1024 * 1024
        ),
        cost_estimate=pl.CostEstimate(
            flops=6 * ticks * order * order * columns,
            bytes_accessed=2 * (10 * order * columns), transcendentals=0,
        ),
    )(down_state, up_state, down_op, up_op, reflect_op, source_bank, ctrl)


def solution(mesh):
    placed = (
        P("layer", None, "shot"),
        P("layer", None, "shot"),
        P("layer", "shot", None),
        P("layer", "shot", None),
        P("layer", "shot", None),
        P("layer", None, None, "shot"),
        P(None, "layer"),
        P("layer"),
    )
    return jax.shard_map(
        functools.partial(body, mesh.shape["layer"], mesh.shape["shot"]),
        mesh=mesh,
        in_specs=placed,
        out_specs=(P("layer", None, "shot"), P("layer", None, "shot")),
        check_vma=False,
    )
```

time: 230 us -> 144 us (0.63)
  Pallas kernels: 0 us -> 138 us
  waiting for transfers between devices: 122 us -> 0 us
  matrix products: 44.5 us -> 0 us
  starting transfers between devices: 27.3 us -> 0 us
  between operations: 21.9 us -> 1.29 us
  local copies, waits for them, and re-layouts: 13 us -> 4 us
    pallas_call x0 -> x1, Pallas kernels: none -> 138 us  [body(): pl.pallas_call(functools.partial(kernel, layers, shots, ticks, batches, c...]
    ppermute x8 -> x0, waiting for transfers between devices: 109 us -> none  [passed_along(): lax.ppermute(value, axis, [(source, source + steps) for source in range(l...]
    dot_general x12 -> x0, matrix products: 44.5 us -> none  [the longest x4 16.4 us: body(): jnp.dot(full_down, down_in, preferred_element_type=jnp.float32)]
    ppermute x8 -> x0, starting transfers between devices: 27.2 us -> none  [passed_along(): lax.ppermute(value, axis, [(source, source + steps) for source in range(l...]
    all_gather x3 -> x0, waiting for transfers between devices: 11.2 us -> none  [the longest x1 11.2 us: body(): lax.all_gather(up_op[0], 'shot', axis=0, tiled=True)]
    unnamed x26 -> x4, local copies, waits for them, and re-layouts: 7.58 us -> 3.32 us
    dynamic_slice x1 -> x0, local copies, waits for them, and re-layouts: 4.04 us -> none  [body(): lax.dynamic_index_in_dim(sources, layer_source[0], 0, keepdims=False)]
  transfers between devices with their start and end apart: 11 -> 0, of which waited for: 5 -> 0; matrix products, arithmetic and copies ran while one was open for 23% -> 0% of each run, Pallas kernels for 0% -> 0%
where the time goes in v1:
time: 144 us
  Pallas kernels  138 us (96%)
  local copies, waits for them, and re-layouts  4 us (3%)
    pallas_call x1, Pallas kernels, body(): pl.pallas_call(functools.partial(kernel, layers, shots, ticks, batches, c...  138 us
    unnamed x4, local copies, waits for them, and re-layouts  3.32 us

profile of v1, /device:TPU:10, one launch (start us, length us, event | category | flops | bytes accessed | tf_op | source)
XLA Modules:
  0.0 144.1 jit_solution(4850945422290570810)
XLA Ops:
  1.3 0.7 pad_add_fusion
  2.0 0.7 broadcast_in_dim.2.ctrl_ref
  2.7 138.1 %shard_map.95 = (bf16[1,1024,512]{2,1,0:T(8,128)(2,1)}, bf16[1,1024,512]{2,1,0:T(8,128)(2,1)}) custom-call(bf16[1,1024,512]{2,1,0:T(8,128)(2,1)} %down_ref.1, bf16[1,1024,512]{2,1,0:T(8,128)(2,1)} %up_ref.1, bf16[1,256,1024]{2,1,0:T(8,128)(2,1)} %dop_ref.1, bf16[1,256,1024]{2,1,0:T(8,128)(2,1)} %uop_ref.1, bf16[1,256,1024]{2,1,0:T(8,128)(2,1)} %rop_ref.1, ...), custom_call_target="tpu_custom_call" | custom-call | flops 12884901888 | bytes 10485760 | tf_op jit(solution)/shard_map/pallas_call | solution.py:301
  140.8 0.0 copy-start
  140.8 2.4 %copy.13 = bf16[1,1024,512]{2,1,0:T(8,128)(2,1)} copy(bf16[1,1024,512]{2,1,0:T(8,128)(2,1)} %get-tuple-element.4) | data formatting | bytes 2097152
  143.1 0.0 copy-done
  143.1 1.0 copy.14
  (1 shorter events, 0.0 us)
Async XLA Ops:
  140.8 2.4 %copy-start = (bf16[1,1024,512]{2,1,0:T(8,128)(2,1)S(1)}, bf16[1,1024,512]{2,1,0:T(8,128)(2,1)}, u32[]{:S(2)}) copy-start(bf16[1,1024,512]{2,1,0:T(8,128)(2,1)} %get-tuple-element.5) | copy-start | bytes 3145732

commit v2 on v1

--- a/solution.py
+++ b/solution.py
@@ -8,7 +8,7 @@
 from jax.sharding import PartitionSpec as P
 
 MESH = pl.DeviceIdType.MESH
-LAG = 2
+LAG = 1
 
 
 def low_bit(mask):
@@ -289,7 +289,7 @@
     ticks, batches = plan.shape[0], source_bank.shape[1]
     width = 256 if columns % 256 == 0 else columns
     chunks = columns // width
-    tile = 256 if order % 256 == 0 else order
+    tile = 512 if order % 512 == 0 else order
     choices = jnp.concatenate([plan[:, 0], layer_source])
     depth = -(-choices.shape[0] // 8) * 8
     ctrl = jnp.broadcast_to(

time: 144 us -> 133 us (0.924); the launches traced: 144 us -> 132 us
  Pallas kernels: 138 us -> 126 us
    pallas_call x1, Pallas kernels: 138 us -> 126 us  [body(): pl.pallas_call(functools.partial(kernel, layers, shots, ticks, batches, c...]
where the time goes in v2:
time: 133 us; the launch traced here: 132 us
  Pallas kernels  126 us (95%)
  local copies, waits for them, and re-layouts  4 us (3%)
    pallas_call x1, Pallas kernels, body(): pl.pallas_call(functools.partial(kernel, layers, shots, ticks, batches, c...  126 us
    unnamed x4, local copies, waits for them, and re-layouts  3.32 us

profile of v2, /device:TPU:10, one launch (start us, length us, event | category | flops | bytes accessed | tf_op | source)
XLA Modules:
  0.0 131.7 jit_solution(3091515273153935987)
XLA Ops:
  1.3 0.7 pad_add_fusion
  2.0 0.7 broadcast_in_dim.2.ctrl_ref
  2.7 125.6 %shard_map.95 = (bf16[1,1024,512]{2,1,0:T(8,128)(2,1)}, bf16[1,1024,512]{2,1,0:T(8,128)(2,1)}) custom-call(bf16[1,1024,512]{2,1,0:T(8,128)(2,1)} %down_ref.1, bf16[1,1024,512]{2,1,0:T(8,128)(2,1)} %up_ref.1, bf16[1,256,1024]{2,1,0:T(8,128)(2,1)} %dop_ref.1, bf16[1,256,1024]{2,1,0:T(8,128)(2,1)} %uop_ref.1, bf16[1,256,1024]{2,1,0:T(8,128)(2,1)} %rop_ref.1, ...), custom_call_target="tpu_custom_call" | custom-call | flops 12884901888 | bytes 10485760 | tf_op jit(solution)/shard_map/pallas_call | solution.py:301
  128.3 0.0 copy-start
  128.3 2.4 %copy.13 = bf16[1,1024,512]{2,1,0:T(8,128)(2,1)} copy(bf16[1,1024,512]{2,1,0:T(8,128)(2,1)} %get-tuple-element.4) | data formatting | bytes 2097152
  130.7 0.0 copy-done
  130.7 1.0 copy.14
  (1 shorter events, 0.0 us)
Async XLA Ops:
  128.3 2.4 %copy-start = (bf16[1,1024,512]{2,1,0:T(8,128)(2,1)S(1)}, bf16[1,1024,512]{2,1,0:T(8,128)(2,1)}, u32[]{:S(2)}) copy-start(bf16[1,1024,512]{2,1,0:T(8,128)(2,1)} %get-tuple-element.5) | copy-start | bytes 3145732
